TPU v7x, 128 devices: a whole 4x4x4 slice. The times are simulated.
128 devices in a mesh: section: 16 (over x, z_hi, core), fsdp: 8 (over z_lo, y).
Axes of the slice: x: 4, y: 4, z: 4 (z_hi: 2, z_lo: 2; z = z_hi * 2 + z_lo), core: 2. Of those that a mesh axis runs over, the one named last changes fastest.
Arguments:
- x_in: bfloat16 [2, 16, 512, 3072], P(None, 'section', 'fsdp'), may hold values from -6 to 6
- expert_ids: int32 [2, 16, 512, 2], P(None, 'section', 'fsdp'), may hold values from 0 to 3, all different within a row; in each aligned block of 64 rows (0 to 63, 64 to 127, ..., all dimensions but the last counted through in order) at most 48 rows name the same one
- out_grad: bfloat16 [2, 16, 512, 3072], P(None, 'section', 'fsdp'), may hold values from -6 to 6
- norm_gain: float32 [2, 16, 3072], P(None, 'section'), may hold values from 0.25 to 1.75
- router: bfloat16 [2, 16, 3072, 4], P(None, 'section'), may hold values from -0.109375 to 0.109375
- w_gate: bfloat16 [2, 16, 3072, 3072], P(None, 'section', None, 'fsdp'), may hold values from -0.109375 to 0.109375
- w_up: bfloat16 [2, 16, 3072, 3072], P(None, 'section', None, 'fsdp'), may hold values from -0.109375 to 0.109375
- w_down: bfloat16 [2, 16, 3072, 3072], P(None, 'section', 'fsdp'), may hold values from -0.21875 to 0.21875
Outputs:
- next_fwd: bfloat16 [2, 16, 512, 3072], P(None, 'section', 'fsdp')
- prev_grad: bfloat16 [2, 16, 512, 3072], P(None, 'section', 'fsdp')
- grad_gate: bfloat16 [16, 3072, 3072], P('section', None, 'fsdp')
- grad_up: bfloat16 [16, 3072, 3072], P('section', None, 'fsdp')
- grad_down: bfloat16 [16, 3072, 3072], P('section', 'fsdp')
- grad_router: bfloat16 [16, 3072, 4], P('section')
Inputs may be any that keep to these rules, and one draw needn't show every extreme that they name: `expert_ids`: the two experts of a token differ. Within one aligned block of 64 rows (one micro-batch's tokens on one device), no expert is named more than 48 times, a bound that some block reaches.
All inputs are finite; a program needn't handle non-finite values.
Results may differ from a plain program's by a relative error of at most 0.024.
Values may be sent and summed in bfloat16 or wider, within the bound.
No kernel may reach another device: no remote copies, remote signals or barrier semaphores. Data moves between devices by JAX's collectives and lax.ppermute only.
A program may use at most 128 MiB of HBM per device.

v0:
```python
import jax
import jax.numpy as jnp
from jax import lax
from jax.sharding import PartitionSpec as P

EPSILON = 1e-05


def shifted(value, axis, steps):
    count = lax.axis_size(axis)
    pairs = [(source, (source + steps) % count) for source in range(count)]
    return lax.ppermute(value, axis, pairs)


def partner(value, axis, distance):
    mask = 2**distance
    pairs = [(source, source ^ mask) for source in range(lax.axis_size(axis))]
    return lax.ppermute(value, axis, pairs)


def normalize(values, scales):
    factor = lax.rsqrt(jnp.mean(values * values, axis=-1, keepdims=True) + EPSILON)
    return values * factor * scales


def routing(picks, experts, capacity):
    count_rows = picks.shape[1]
    expert_lanes = jnp.arange(experts, dtype=jnp.int32)
    first_pick = (picks[..., 0:1] == expert_lanes).astype(jnp.float32)
    second_pick = (picks[..., 1:2] == expert_lanes).astype(jnp.float32)
    row_index = jnp.arange(count_rows, dtype=jnp.int32)
    before = (row_index[None, :] < row_index[:, None]).astype(jnp.float32)
    earlier = jnp.einsum("tu,bue->bte", before, first_pick + second_pick)
    offsets = earlier + capacity * expert_lanes.astype(jnp.float32)
    first_slot = jnp.sum(first_pick * offsets, axis=-1)
    second_slot = jnp.sum(second_pick * offsets, axis=-1)
    slot_lanes = jnp.arange(experts * capacity, dtype=jnp.int32).astype(jnp.float32)
    first_place = (slot_lanes[None, :, None] == first_slot[:, None, :]).astype(jnp.float32)
    second_place = (slot_lanes[None, :, None] == second_slot[:, None, :]).astype(jnp.float32)
    return (first_pick, second_pick, first_place, second_place)


def mirror_add(own, other):
    kept = lax.optimization_barrier(own.astype(jnp.bfloat16))
    return (kept.astype(jnp.float32) + other.astype(jnp.float32)).astype(jnp.bfloat16)


def on_device(x_in, expert_ids, out_grad, norm_gain, router, w_gate, w_up, w_down):
    section_rows = x_in[:, 0]
    picks = expert_ids[:, 0]
    upstream = out_grad[:, 0]
    scales = norm_gain[:, 0][:, None, :]
    mixer = router[:, 0]
    gate_mat = w_gate[:, 0]
    up_mat = w_up[:, 0]
    down_mat = w_down[:, 0]
    token_count = section_rows.shape[1]
    model_width = section_rows.shape[2]
    experts = mixer.shape[2]
    capacity = 3 * token_count // 4
    slot_count = experts * capacity
    group_count = lax.axis_size("fsdp")
    sharers = group_count // experts

    def spread_out(slots):
        copies = jnp.broadcast_to(
            slots.reshape(2, experts, 1, capacity, model_width),
            (2, experts, sharers, capacity, model_width),
        )
        return copies.reshape(2, group_count, capacity, model_width)

    def fold_back(pieces):
        parts = pieces.reshape(2, experts, sharers, capacity, model_width).astype(jnp.float32)
        return jnp.sum(parts, axis=2).reshape(2, slot_count, model_width)

    first_pick, second_pick, first_place, second_place = routing(picks, experts, capacity)
    both_place = first_place + second_place
    both_half = both_place.astype(jnp.bfloat16)
    inputs_wide = section_rows.astype(jnp.float32)
    normed = normalize(inputs_wide, scales).astype(jnp.bfloat16)
    logits = jnp.einsum("ctd,cde->cte", normed, mixer, preferred_element_type=jnp.float32)
    first_weight = jax.nn.sigmoid(jnp.sum((first_pick - second_pick) * logits, axis=-1))
    second_weight = 1.0 - first_weight
    outgoing = jnp.einsum(
        "cst,ctd->csd", both_half, normed, preferred_element_type=jnp.float32
    ).astype(jnp.bfloat16)
    arrived = lax.all_to_all(spread_out(outgoing), "fsdp", split_axis=1, concat_axis=1, tiled=True)
    arrived = arrived.reshape(2, group_count * capacity, model_width)
    gate_pre = jnp.einsum("csd,cdf->csf", arrived, gate_mat, preferred_element_type=jnp.float32)
    up_pre = jnp.einsum("csd,cdf->csf", arrived, up_mat, preferred_element_type=jnp.float32)
    sigmoid_gate = jax.nn.sigmoid(gate_pre)
    activated = gate_pre * sigmoid_gate
    hidden = (activated * up_pre).astype(jnp.bfloat16)
    part_out = jnp.einsum(
        "csf,cfd->csd", hidden, down_mat, preferred_element_type=jnp.float32
    ).astype(jnp.bfloat16)
    returned = lax.all_to_all(
        part_out.reshape(2, group_count, capacity, model_width),
        "fsdp",
        split_axis=1,
        concat_axis=1,
        tiled=True,
    )
    returned = fold_back(returned)
    first_out = jnp.einsum("cst,csd->ctd", first_place, returned)
    second_out = jnp.einsum("cst,csd->ctd", second_place, returned)
    section_out = (
        inputs_wide + first_weight[..., None] * first_out + second_weight[..., None] * second_out
    ).astype(jnp.bfloat16)
    down_next = shifted(section_out[0], "section", 1)
    up_next = shifted(section_out[1], "section", -1)
    upstream_wide = upstream.astype(jnp.float32)
    slot_weight = jnp.einsum("cst,ct->cs", first_place, first_weight) + jnp.einsum(
        "cst,ct->cs", second_place, second_weight
    )
    picked = jnp.einsum("cst,ctd->csd", both_half, upstream, preferred_element_type=jnp.float32)
    expert_grad = (picked * slot_weight[..., None]).astype(jnp.bfloat16)
    grad_arrived = lax.all_to_all(
        spread_out(expert_grad), "fsdp", split_axis=1, concat_axis=1, tiled=True
    )
    grad_arrived = grad_arrived.reshape(2, group_count * capacity, model_width)
    hidden_grad = jnp.einsum(
        "csd,cfd->csf", grad_arrived, down_mat, preferred_element_type=jnp.float32
    )
    gate_slope = sigmoid_gate * (1.0 + gate_pre * (1.0 - sigmoid_gate))
    gate_pre_grad = (hidden_grad * up_pre * gate_slope).astype(jnp.bfloat16)
    up_pre_grad = (hidden_grad * activated).astype(jnp.bfloat16)
    down_total = jnp.einsum(
        "csf,csd->cfd", hidden, grad_arrived, preferred_element_type=jnp.float32
    )
    gate_total = jnp.einsum(
        "csd,csf->cdf", arrived, gate_pre_grad, preferred_element_type=jnp.float32
    )
    up_total = jnp.einsum("csd,csf->cdf", arrived, up_pre_grad, preferred_element_type=jnp.float32)
    part_normed = (
        jnp.einsum("csf,cdf->csd", gate_pre_grad, gate_mat, preferred_element_type=jnp.float32)
        + jnp.einsum("csf,cdf->csd", up_pre_grad, up_mat, preferred_element_type=jnp.float32)
    ).astype(jnp.bfloat16)
    normed_back = lax.all_to_all(
        part_normed.reshape(2, group_count, capacity, model_width),
        "fsdp",
        split_axis=1,
        concat_axis=1,
        tiled=True,
    )
    normed_back = fold_back(normed_back)
    normed_grad = jnp.einsum("cst,csd->ctd", both_place, normed_back)
    first_dot = jnp.sum(upstream_wide * first_out, axis=-1)
    second_dot = jnp.sum(upstream_wide * second_out, axis=-1)
    logit_grad = (first_dot - second_dot) * first_weight * second_weight
    logits_grad = ((first_pick - second_pick) * logit_grad[..., None]).astype(jnp.bfloat16)
    normed_grad = normed_grad + jnp.einsum(
        "cte,cde->ctd", logits_grad, mixer, preferred_element_type=jnp.float32
    )
    router_local = jnp.einsum(
        "ctd,cte->cde", normed, logits_grad, preferred_element_type=jnp.float32
    )
    router_total = lax.psum(router_local.astype(jnp.bfloat16), "fsdp").astype(jnp.float32)
    _, pullback = jax.vjp(lambda values: normalize(values, scales), inputs_wide)
    input_grad = (upstream_wide + pullback(normed_grad)[0]).astype(jnp.bfloat16)
    down_back = shifted(input_grad[0], "section", -1)
    up_back = shifted(input_grad[1], "section", 1)
    levels = lax.axis_size("section").bit_length() - 1
    gate_far = gate_total[1].astype(jnp.bfloat16)
    up_far = up_total[1].astype(jnp.bfloat16)
    down_far = down_total[1].astype(jnp.bfloat16)
    router_far = router_total[1].astype(jnp.bfloat16)
    for level in range(levels):
        gate_far, up_far, down_far, router_far = partner(
            (gate_far, up_far, down_far, router_far), "section", level
        )
    grad_gate = mirror_add(gate_total[0], gate_far)[None]
    grad_up = mirror_add(up_total[0], up_far)[None]
    grad_down = mirror_add(down_total[0], down_far)[None]
    grad_router = mirror_add(router_total[0], router_far)[None]
    next_fwd = jnp.stack([down_next, up_next])[:, None]
    prev_grad = jnp.stack([down_back, up_back])[:, None]
    return (next_fwd, prev_grad, grad_gate, grad_up, grad_down, grad_router)


def solution(mesh):
    in_specs = (
        P(None, "section", "fsdp", None),
        P(None, "section", "fsdp", None),
        P(None, "section", "fsdp", None),
        P(None, "section", None),
        P(None, "section", None, None),
        P(None, "section", None, "fsdp"),
        P(None, "section", None, "fsdp"),
        P(None, "section", "fsdp", None),
    )
    out_specs = (
        P(None, "section", "fsdp", None),
        P(None, "section", "fsdp", None),
        P("section", None, "fsdp"),
        P("section", None, "fsdp"),
        P("section", "fsdp", None),
        P("section", None, None),
    )
    return jax.shard_map(
        on_device, mesh=mesh, in_specs=in_specs, out_specs=out_specs, check_vma=False
    )
```

profile of v0, /device:TPU:6, one launch (start us, length us, event | category | flops | bytes accessed | tf_op | source)
XLA Modules:
  0.0 743.5 jit_solution(7272749291016508039)
XLA Ops:
  0.7 0.8 fusion.73
  1.4 1.4 fusion.17
  2.8 0.8 copy.69
  3.7 2.1 convolution_convert_fusion.4
  5.9 0.6 broadcast_in_dim.23
  6.5 61.2 %all_to_all.20 = bf16[2,8,48,3072]{3,2,0,1:T(8,128)(2,1)S(1)} all-to-all(bf16[2,8,48,3072]{3,2,0,1:T(8,128)(2,1)S(1)} %bitcast.155), channel_id=1, replica_groups=mesh['section'=16,'fsdp'=8] {'fsdp'}, dimensions={1} | all-to-all | bytes 9437184 | tf_op jit(solution)/shard_map/all_to_all | solution.py:87
  68.2 0.6 slice-done.3
  68.8 2.6 fusion.8
  71.9 3.7 multiply_convert_fusion.3
  75.6 2.9 convolution_convert_fusion.3
  78.5 2.6 copy.47
  81.1 4.8 all-to-all-start.1
  86.3 53.4 %all-to-all-done.1 = bf16[2,8,48,3072]{3,2,0,1:T(8,128)(2,1)} async-done(((bf16[2,8,48,3072]{3,2,0,1:T(8,128)(2,1)}), bf16[2,8,48,3072]{3,2,0,1:T(8,128)(2,1)}, u32[]{:S(2)}, u32[]{:S(2)}) %all-to-all-start.1) | async-done | bytes 4718624 | tf_op jit(solution)/shard_map/all_to_all | solution.py:97
  139.7 3.7 convert_reduce_fusion.1
  143.6 0.6 fusion.36
  144.2 0.5 copy-done.7
  144.7 2.1 fusion.15
  147.2 0.9 multiply_convert_fusion
  148.3 0.6 broadcast_in_dim.26
  148.9 68.5 %all_to_all.21 = bf16[2,8,48,3072]{3,2,0,1:T(8,128)(2,1)S(1)} all-to-all(bf16[2,8,48,3072]{3,2,0,1:T(8,128)(2,1)S(1)} %bitcast.156), channel_id=1, replica_groups=mesh['section'=16,'fsdp'=8] {'fsdp'}, dimensions={1} | all-to-all | bytes 9437184 | tf_op jit(solution)/shard_map/all_to_all | solution.py:118
  217.8 0.6 copy-done.10
  218.4 2.9 convolution_convert_fusion
  221.3 2.7 slice_bitcast_fusion.1
  224.1 3.7 multiply_convert_fusion.1
  227.8 3.4 convolution_convert_fusion.1
  231.2 2.7 slice_bitcast_fusion.3
  233.9 0.6 collective-permute-start.8
  234.5 4.5 fusion.6
  239.1 7.4 add_convert_fusion
  246.5 6.0 convolution_convert_fusion.2
  252.5 2.6 copy.51
  255.1 4.6 all-to-all-start.3
  259.7 4.3 slice_bitcast_fusion.5
  264.0 3.6 collective-permute-start.13
  267.7 1.0 collective-permute-done.4
  268.6 3.6 collective-permute-start.5
  272.6 82.1 %psum.7 = bf16[2,3072,4]{1,2,0:T(4,128)(2,1)S(1)} all-reduce(bf16[2,3072,4]{1,2,0:T(4,128)(2,1)S(1)} %convolution_convert_fusion.5), channel_id=1, replica_groups=mesh['section'=16,'fsdp'=8] {'fsdp'}, use_global_device_ids=true, to_apply=%region_9.0 | all-reduce | flops 24576 | bytes 98304 | tf_op jit(solution)/shard_map/psum | solution.py:158
  354.7 12.8 %collective-permute-done.13 = bf16[384,3072]{1,0:T(8,128)(2,1)} collective-permute-done((bf16[384,3072]{1,0:T(8,128)(2,1)}, bf16[384,3072]{1,0:T(8,128)(2,1)}, u32[]{:S(2)}, u32[]{:S(2)}) %collective-permute-start.13) | collective-permute-done | bytes 2359328 | tf_op jit(solution)/shard_map/ppermute | solution.py:18
  367.5 0.8 collective-permute-start.14
  368.4 1.2 collective-permute-done.16
  369.6 98.8 %collective-permute-done.17 = bf16[3072,4]{0,1:T(4,128)(2,1)S(1)} collective-permute-done((bf16[3072,4]{0,1:T(4,128)(2,1)S(1)}, bf16[3072,4]{0,1:T(4,128)(2,1)S(1)}, u32[]{:S(2)}, u32[]{:S(2)}) %collective-permute-start.17) | collective-permute-done | bytes 24608 | tf_op jit(solution)/shard_map/ppermute | solution.py:18
  468.4 0.8 collective-permute-start.18
  469.2 3.0 collective-permute-done.18
  472.3 1.4 collective-permute-start.19
  473.7 3.7 convert_reduce_fusion
  477.6 0.6 fusion.39
  478.2 0.6 fusion.22
  478.9 2.3 collective-permute-start.6
  481.2 0.9 fusion.16
  482.1 2.2 collective-permute-start.15
  484.9 47.1 %collective-permute-done.10 = bf16[3072,384]{1,0:T(8,128)(2,1)S(1)} collective-permute-done((bf16[3072,384]{1,0:T(8,128)(2,1)}, bf16[3072,384]{1,0:T(8,128)(2,1)S(1)}, u32[]{:S(2)}, u32[]{:S(2)}) %collective-permute-start.10) | collective-permute-done | bytes 2359328 | tf_op jit(solution)/shard_map/ppermute | solution.py:18
  532.0 2.1 collective-permute-start.11
  534.2 104.9 %collective-permute-done.2 = bf16[64,3072]{1,0:T(8,128)(2,1)S(1)} collective-permute-done((bf16[64,3072]{1,0:T(8,128)(2,1)S(1)}, bf16[64,3072]{1,0:T(8,128)(2,1)S(1)}, u32[]{:S(2)}, u32[]{:S(2)}) %collective-permute-start.2) | collective-permute-done | bytes 393248 | tf_op jit(solution)/shard_map/ppermute | solution.py:12
  639.1 4.3 collective-permute-start.1
  643.4 0.6 fusion.65
  644.0 3.8 collective-permute-start.7
  647.8 0.9 maximum_bitcast_fusion.1
  648.8 45.4 %collective-permute-done = bf16[64,3072]{1,0:T(8,128)(2,1)S(1)} collective-permute-done((bf16[64,3072]{1,0:T(8,128)(2,1)S(1)}, bf16[64,3072]{1,0:T(8,128)(2,1)S(1)}, u32[]{:S(2)}, u32[]{:S(2)}) %collective-permute-start) | collective-permute-done | bytes 393248 | tf_op jit(solution)/shard_map/ppermute | solution.py:12
  694.2 3.8 collective-permute-done.1
  698.1 0.9 maximum_bitcast_fusion
  699.0 2.3 fusion.13
  701.3 2.0 fusion.12
  703.3 38.0 %collective-permute-done.7 = bf16[3072,384]{1,0:T(8,128)(2,1)S(1)} collective-permute-done((bf16[3072,384]{1,0:T(8,128)(2,1)S(1)}, bf16[3072,384]{1,0:T(8,128)(2,1)S(1)}, u32[]{:S(2)}, u32[]{:S(2)}) %collective-permute-start.7) | collective-permute-done | bytes 2359328 | tf_op jit(solution)/shard_map/ppermute | solution.py:18
  741.3 2.0 fusion.11
  (95 shorter events, 4.5 us)
Async XLA Ops:
  0.6 85.3 %copy-start = (bf16[2,1,3072,4]{2,3,1,0:T(4,128)(2,1)S(1)}, bf16[2,1,3072,4]{2,3,1,0:T(4,128)(2,1)}, u32[]{:S(2)}) copy-start(bf16[2,1,3072,4]{2,3,1,0:T(4,128)(2,1)} %param.12) | copy-start | bytes 147460
  6.5 61.7 %slice-start.2 = ((s8[4718592]{0:T(1024)(128)(4,1)}), s8[4194304]{0:T(1024)(128)(4,1)S(1)}, s32[]{:S(2)}) async-start(s8[4718592]{0:T(1024)(128)(4,1)} %bitcast.161), calls=%async_computation.6 | async-start | bytes 8388608
  67.7 1.0 slice-start.3
  67.7 4.1 slice-start.8
  68.2 3.2 copy-start.1
  68.8 3.1 slice-start.9
  68.8 6.8 slice-start.4
  71.9 3.7 copy-start.13
  71.9 3.7 slice-start.5
  75.6 2.9 copy-start.9
  81.1 4.8 copy-start.3
  81.1 58.6 %all-to-all-start.1 = ((bf16[2,8,48,3072]{3,2,0,1:T(8,128)(2,1)}), bf16[2,8,48,3072]{3,2,0,1:T(8,128)(2,1)}, u32[]{:S(2)}, u32[]{:S(2)}) async-start(bf16[2,8,48,3072]{3,2,0,1:T(8,128)(2,1)} %copy.47), calls=%async_computation.1 | async-start | bytes 9437184 | tf_op jit(solution)/shard_map/all_to_all | solution.py:97
  143.6 1.1 copy-start.7
  217.3 1.1 copy-start.10
  217.3 6.7 slice-start.6
  218.4 5.7 slice-start.7
  221.3 2.8 copy-start.14
  221.3 2.8 copy-start.15
  221.3 6.5 slice-start
  224.0 40.0 %collective-permute-start.12 = (bf16[384,3072]{1,0:T(8,128)(2,1)}, bf16[384,3072]{1,0:T(8,128)(2,1)}, u32[]{:S(2)}, u32[]{:S(2)}) collective-permute-start(bf16[384,3072]{1,0:T(8,128)(2,1)} %get-tuple-element.37), channel_id=1, source_target_pairs={{0,8},{8,0},{16,24},{24,16},{32,40},{40,32},{48,56},{56,48},{64,72... | collective-permute-start | bytes 7077896 | tf_op jit(solution)/shard_map/ppermute | solution.py:18
  224.1 3.7 slice-start.1
  227.8 3.4 copy-start.12
  231.2 3.3 copy-start.11
  233.9 33.7 %collective-permute-start.8 = (bf16[3072,384]{1,0:T(8,128)(2,1)}, bf16[3072,384]{1,0:T(8,128)(2,1)}, u32[]{:S(2)}, u32[]{:S(2)}) collective-permute-start(bf16[3072,384]{1,0:T(8,128)(2,1)} %get-tuple-element.39), channel_id=1, source_target_pairs={{0,8},{8,0},{16,24},{24,16},{32,40},{40,32},{48,56},{56,48},{64,72... | collective-permute-start | bytes 7077896 | tf_op jit(solution)/shard_map/ppermute | solution.py:18
  246.5 6.0 copy-start.2
  255.1 218.6 %all-to-all-start.3 = ((bf16[2,8,48,3072]{3,2,0,1:T(8,128)(2,1)}), bf16[2,8,48,3072]{3,2,0,1:T(8,128)(2,1)}, u32[]{:S(2)}, u32[]{:S(2)}) async-start(bf16[2,8,48,3072]{3,2,0,1:T(8,128)(2,1)} %copy.51), calls=%async_computation.3 | async-start | bytes 9437184 | tf_op jit(solution)/shard_map/all_to_all | solution.py:139
  264.0 4.7 collective-permute-start.4
  264.0 103.5 %collective-permute-start.13 = (bf16[384,3072]{1,0:T(8,128)(2,1)}, bf16[384,3072]{1,0:T(8,128)(2,1)}, u32[]{:S(2)}, u32[]{:S(2)}) collective-permute-start(bf16[384,3072]{1,0:T(8,128)(2,1)} %collective-permute-done.12), channel_id=1, source_target_pairs={{0,16},{8,24},{16,0},{24,8},{32,48},{40,56},{48,32},{56,40},{64,80... | collective-permute-start | bytes 7077896 | tf_op jit(solution)/shard_map/ppermute | solution.py:18
  267.6 209.9 %collective-permute-start.9 = (bf16[3072,384]{1,0:T(8,128)(2,1)}, bf16[3072,384]{1,0:T(8,128)(2,1)}, u32[]{:S(2)}, u32[]{:S(2)}) collective-permute-start(bf16[3072,384]{1,0:T(8,128)(2,1)} %collective-permute-done.8), channel_id=1, source_target_pairs={{0,16},{8,24},{16,0},{24,8},{32,48},{40,56},{48,32},{56,40},{64,80... | collective-permute-start | bytes 7077896 | tf_op jit(solution)/shard_map/ppermute | solution.py:18
  268.6 210.2 %collective-permute-start.5 = (bf16[3072,384]{1,0:T(8,128)(2,1)}, bf16[3072,384]{1,0:T(8,128)(2,1)}, u32[]{:S(2)}, u32[]{:S(2)}) collective-permute-start(bf16[3072,384]{1,0:T(8,128)(2,1)} %collective-permute-done.4), channel_id=1, source_target_pairs={{0,16},{8,24},{16,0},{24,8},{32,48},{40,56},{48,32},{56,40},{64,80... | collective-permute-start | bytes 7077896 | tf_op jit(solution)/shard_map/ppermute | solution.py:18
  367.5 114.5 %collective-permute-start.14 = (bf16[384,3072]{1,0:T(8,128)(2,1)}, bf16[384,3072]{1,0:T(8,128)(2,1)}, u32[]{:S(2)}, u32[]{:S(2)}) collective-permute-start(bf16[384,3072]{1,0:T(8,128)(2,1)} %collective-permute-done.13), channel_id=1, source_target_pairs={{0,32},{8,40},{16,48},{24,56},{32,0},{40,8},{48,16},{56,24},{64,96... | collective-permute-start | bytes 7077896 | tf_op jit(solution)/shard_map/ppermute | solution.py:18
  368.3 1.3 collective-permute-start.16
  369.6 98.8 %collective-permute-start.17 = (bf16[3072,4]{0,1:T(4,128)(2,1)S(1)}, bf16[3072,4]{0,1:T(4,128)(2,1)S(1)}, u32[]{:S(2)}, u32[]{:S(2)}) collective-permute-start(bf16[3072,4]{0,1:T(4,128)(2,1)S(1)} %collective-permute-done.16), channel_id=1, source_target_pairs={{0,16},{8,24},{16,0},{24,8},{32,48},{40,56},{48,32},{56,40},{64,80... | collective-permute-start | bytes 73736 | tf_op jit(solution)/shard_map/ppermute | solution.py:18
  468.4 3.8 collective-permute-start.18
  472.3 12.2 %collective-permute-start.19 = (bf16[3072,4]{0,1:T(4,128)(2,1)S(1)}, bf16[3072,4]{0,1:T(4,128)(2,1)S(1)}, u32[]{:S(2)}, u32[]{:S(2)}) collective-permute-start(bf16[3072,4]{0,1:T(4,128)(2,1)S(1)} %collective-permute-done.18), channel_id=1, source_target_pairs={{0,64},{8,72},{16,80},{24,88},{32,96},{40,104},{48,112},{56,120},{... | collective-permute-start | bytes 73736 | tf_op jit(solution)/shard_map/ppermute | solution.py:18
  477.5 54.5 %collective-permute-start.10 = (bf16[3072,384]{1,0:T(8,128)(2,1)}, bf16[3072,384]{1,0:T(8,128)(2,1)S(1)}, u32[]{:S(2)}, u32[]{:S(2)}) collective-permute-start(bf16[3072,384]{1,0:T(8,128)(2,1)} %collective-permute-done.9), channel_id=1, source_target_pairs={{0,32},{8,40},{16,48},{24,56},{32,0},{40,8},{48,16},{56,24},{64,96... | collective-permute-start | bytes 7077896 | tf_op jit(solution)/shard_map/ppermute | solution.py:18
  478.2 2.9 copy-start.8
  478.9 165.1 %collective-permute-start.6 = (bf16[3072,384]{1,0:T(8,128)(2,1)}, bf16[3072,384]{1,0:T(8,128)(2,1)S(1)}, u32[]{:S(2)}, u32[]{:S(2)}) collective-permute-start(bf16[3072,384]{1,0:T(8,128)(2,1)} %collective-permute-done.5), channel_id=1, source_target_pairs={{0,32},{8,40},{16,48},{24,56},{32,0},{40,8},{48,16},{56,24},{64,96... | collective-permute-start | bytes 7077896 | tf_op jit(solution)/shard_map/ppermute | solution.py:18
  482.1 216.9 %collective-permute-start.15 = (bf16[384,3072]{1,0:T(8,128)(2,1)}, bf16[384,3072]{1,0:T(8,128)(2,1)S(1)}, u32[]{:S(2)}, u32[]{:S(2)}) collective-permute-start(bf16[384,3072]{1,0:T(8,128)(2,1)} %collective-permute-done.14), channel_id=1, source_target_pairs={{0,64},{8,72},{16,80},{24,88},{32,96},{40,104},{48,112},{56,120},{... | collective-permute-start | bytes 7077896 | tf_op jit(solution)/shard_map/ppermute | solution.py:18
  484.3 154.7 %collective-permute-start.2 = (bf16[64,3072]{1,0:T(8,128)(2,1)S(1)}, bf16[64,3072]{1,0:T(8,128)(2,1)S(1)}, u32[]{:S(2)}, u32[]{:S(2)}) collective-permute-start(bf16[64,3072]{1,0:T(8,128)(2,1)S(1)} %get-tuple-element.44), channel_id=1, source_target_pairs={{0,120},{8,0},{16,8},{24,16},{32,24},{40,32},{48,40},{56,48},{64,5... | collective-permute-start | bytes 1179656 | tf_op jit(solution)/shard_map/ppermute | solution.py:12
  484.4 154.6 %collective-permute-start.3 = (bf16[64,3072]{1,0:T(8,128)(2,1)S(1)}, bf16[64,3072]{1,0:T(8,128)(2,1)S(1)}, u32[]{:S(2)}, u32[]{:S(2)}) collective-permute-start(bf16[64,3072]{1,0:T(8,128)(2,1)S(1)} %get-tuple-element.45), channel_id=1, source_target_pairs={{0,8},{8,16},{16,24},{24,32},{32,40},{40,48},{48,56},{56,64},{64,7... | collective-permute-start | bytes 1179656 | tf_op jit(solution)/shard_map/ppermute | solution.py:12
  532.0 169.3 %collective-permute-start.11 = (bf16[3072,384]{1,0:T(8,128)(2,1)S(1)}, bf16[3072,384]{1,0:T(8,128)(2,1)S(1)}, u32[]{:S(2)}, u32[]{:S(2)}) collective-permute-start(bf16[3072,384]{1,0:T(8,128)(2,1)S(1)} %collective-permute-done.10), channel_id=1, source_target_pairs={{0,64},{8,72},{16,80},{24,88},{32,96},{40,104},{48,112},{56,120},{... | collective-permute-start | bytes 7077896 | tf_op jit(solution)/shard_map/ppermute | solution.py:18
  534.1 164.9 %copy-start.4 = (bf16[384,3072]{1,0:T(8,128)(2,1)S(1)}, bf16[384,3072]{1,0:T(8,128)(2,1)}, u32[]{:S(2)}) copy-start(bf16[384,3072]{1,0:T(8,128)(2,1)} %get-tuple-element.36) | copy-start | bytes 7077892
  639.1 55.2 %collective-permute-start = (bf16[64,3072]{1,0:T(8,128)(2,1)S(1)}, bf16[64,3072]{1,0:T(8,128)(2,1)S(1)}, u32[]{:S(2)}, u32[]{:S(2)}) collective-permute-start(bf16[64,3072]{1,0:T(8,128)(2,1)S(1)} %get-tuple-element.48), channel_id=1, source_target_pairs={{0,8},{8,16},{16,24},{24,32},{32,40},{40,48},{48,56},{56,64},{64,7... | collective-permute-start | bytes 1179656 | tf_op jit(solution)/shard_map/ppermute | solution.py:12
  639.1 59.0 %collective-permute-start.1 = (bf16[64,3072]{1,0:T(8,128)(2,1)S(1)}, bf16[64,3072]{1,0:T(8,128)(2,1)S(1)}, u32[]{:S(2)}, u32[]{:S(2)}) collective-permute-start(bf16[64,3072]{1,0:T(8,128)(2,1)S(1)} %get-tuple-element.49), channel_id=1, source_target_pairs={{0,120},{8,0},{16,8},{24,16},{32,24},{40,32},{48,40},{56,48},{64,5... | collective-permute-start | bytes 1179656 | tf_op jit(solution)/shard_map/ppermute | solution.py:12
  644.0 97.3 %collective-permute-start.7 = (bf16[3072,384]{1,0:T(8,128)(2,1)S(1)}, bf16[3072,384]{1,0:T(8,128)(2,1)S(1)}, u32[]{:S(2)}, u32[]{:S(2)}) collective-permute-start(bf16[3072,384]{1,0:T(8,128)(2,1)S(1)} %collective-permute-done.6), channel_id=1, source_target_pairs={{0,64},{8,72},{16,80},{24,88},{32,96},{40,104},{48,112},{56,120},{... | collective-permute-start | bytes 7077896 | tf_op jit(solution)/shard_map/ppermute | solution.py:18
  699.0 2.3 copy-start.5
  701.3 40.0 %copy-start.6 = (bf16[3072,384]{1,0:T(8,128)(2,1)S(1)}, bf16[3072,384]{1,0:T(8,128)(2,1)}, u32[]{:S(2)}) copy-start(bf16[3072,384]{1,0:T(8,128)(2,1)} %get-tuple-element.40) | copy-start | bytes 7077892
where the time goes:
time: 753 us; the launch traced here: 744 us
  waiting for transfers between devices  410 us (54%)
  blocking collectives  212 us (28%)
  matrix products  45.2 us (6%)
  starting transfers between devices  35.8 us (5%)
  local copies, waits for them, and re-layouts  21.5 us (3%)
  other arithmetic  18.5 us (2%)
    ppermute x16, waiting for transfers between devices, partner(): return lax.ppermute(value, axis, pairs)  202 us
    ppermute x4, waiting for transfers between devices, shifted(): return lax.ppermute(value, axis, pairs)  154 us
    psum x1, blocking collectives, on_device(): lax.psum(router_local.astype(jnp.bfloat16), 'fsdp').astype(jnp.float32)  82.1 us
    all_to_all x1, blocking collectives, on_device(): lax.all_to_all(spread_out(expert_grad), 'fsdp', split_axis=1, concat_axis...  68.5 us
    all_to_all x1, blocking collectives, on_device(): lax.all_to_all(spread_out(outgoing), 'fsdp', split_axis=1, concat_axis=1,...  61.2 us
    all_to_all x1, waiting for transfers between devices, on_device(): lax.all_to_all(part_out.reshape(2, group_count, capacity, model_width), '...  53.4 us
    ppermute x16, starting transfers between devices, partner(): return lax.ppermute(value, axis, pairs)  21.5 us
  transfers between devices with their start and end apart: 22, of which 11 were waited for; matrix products, arithmetic and copies ran while one was open for 6% of the time, Pallas kernels for 0%

commit v1 on v0

v1 whole, which is shorter than its diff:
```python
import jax
import jax.numpy as jnp
from jax import lax
from jax.sharding import PartitionSpec as P

EPSILON = 1e-05
RING = 4
BF16 = jnp.bfloat16
F32 = jnp.float32


def permuted(value, axis, target):
    pairs = [(source, target(source)) for source in range(lax.axis_size(axis))]
    return lax.ppermute(value, axis, pairs)


def shifted(value, steps):
    count = lax.axis_size("section")
    return permuted(value, "section", lambda s: (s + steps) % count)


def mirrored(value):
    count = lax.axis_size("section")
    return permuted(value, "section", lambda s: count - 1 - s)


def ring(value, steps):
    return permuted(value, "fsdp", lambda s: s // RING * RING + (s + steps) % RING)


def across(value):
    return permuted(value, "fsdp", lambda s: s ^ RING)


def flipped(value, mask):
    return permuted(value, "fsdp", lambda s: s ^ mask)


def add_half(first, second):
    return (first.astype(F32) + second.astype(F32)).astype(BF16)


def gather_rows(own):
    half = own.shape[0]
    pair = jnp.concatenate([own, across(own)])
    from_left = ring(pair, 1)
    from_right = ring(pair, -1)
    far_own = ring(from_left[:half], 1)
    far_other = ring(from_right[half:], -1)
    return jnp.concatenate([pair, from_left, from_right, far_own, far_other])


def scatter_rows(partial):
    half = partial.shape[0] // 8
    mine, left, right, far = [partial[2 * half * i : 2 * half * (i + 1)] for i in range(4)]
    far_own = ring(far[:half], 1)
    far_other = ring(far[half:], -1)
    right = jnp.concatenate([add_half(right[:half], far_own), right[half:]])
    left = jnp.concatenate([left[:half], add_half(left[half:], far_other)])
    from_left = ring(right, 1)
    from_right = ring(left, -1)
    total = mine.astype(F32) + from_left.astype(F32) + from_right.astype(F32)
    return total[:half] + across(total[half:].astype(BF16)).astype(F32)


def gather_small(own):
    pair = jnp.stack([own, across(own)])
    near = flipped(pair, 1)
    quad = jnp.stack([pair, near])
    far = flipped(quad, 2)
    odd = lax.axis_index("fsdp") % 2 == 1
    before = jnp.where(odd, near, far[1])
    after = jnp.where(odd, far[1], near)
    return jnp.concatenate([pair, before, after, far[0]])


def sum_small(own):
    for mask in (RING, 1, 2):
        own = own + flipped(own, mask)
    return own


def normalize(values, scales):
    factor = lax.rsqrt(jnp.mean(values * values, axis=-1, keepdims=True) + EPSILON)
    return values * factor * scales


def dot(first, second, contract):
    return lax.dot_general(first, second, (contract, ((), ())), preferred_element_type=F32)


def on_device(x_in, expert_ids, out_grad, norm_gain, router, w_gate, w_up, w_down):
    experts = router.shape[3]
    sharers = lax.axis_size("fsdp") // experts
    my_expert = (jnp.arange(experts) == lax.axis_index("fsdp") // sharers).astype(F32)

    normed, extras = [], []
    for c in range(2):
        picks = expert_ids[c, 0]
        lanes = jnp.arange(experts, dtype=jnp.int32)
        first_pick = (picks[:, 0:1] == lanes).astype(F32)
        second_pick = (picks[:, 1:2] == lanes).astype(F32)
        sign = first_pick - second_pick
        rows = normalize(x_in[c, 0].astype(F32), norm_gain[c, 0]).astype(BF16)
        logits = dot(rows, router[c, 0], ((1,), (0,)))
        first_weight = jax.nn.sigmoid(jnp.sum(sign * logits, axis=-1, keepdims=True))
        second_weight = 1.0 - first_weight
        weights = first_pick * first_weight + second_pick * second_weight
        slopes = first_weight * second_weight * sign
        normed.append(rows)
        extras.append(jnp.concatenate([weights.T, sign.T, slopes.T]))
    extras = gather_small(jnp.stack(extras))

    outs, backs, pre_grads, downs, routers, rows_all = {}, {}, {}, {}, {}, {}
    for c in (1, 0):
        upstream = gather_rows(out_grad[c, 0])
        rows = gather_rows(normed[c])
        rows_all[c] = rows
        small = extras[:, c].transpose(0, 2, 1).reshape(-1, 3 * experts)
        weight = jnp.sum(small[:, :experts] * my_expert, axis=-1, keepdims=True)
        sign = small[:, experts : 2 * experts]
        slope = jnp.sum(small[:, 2 * experts :] * my_expert, axis=-1, keepdims=True)
        gate_mat, up_mat, down_mat = w_gate[c, 0], w_up[c, 0], w_down[c, 0]
        gate_pre = dot(rows, gate_mat, ((1,), (0,)))
        up_pre = dot(rows, up_mat, ((1,), (0,)))
        sigmoid_gate = jax.nn.sigmoid(gate_pre)
        activated = gate_pre * sigmoid_gate
        hidden = (activated * up_pre).astype(BF16)
        raw_grad = dot(upstream, down_mat, ((1,), (1,)))
        outs[c] = (dot(hidden, down_mat, ((1,), (0,))) * weight).astype(BF16)
        gate_slope = sigmoid_gate * (1.0 + gate_pre * (1.0 - sigmoid_gate))
        hidden_grad = raw_grad * weight
        gate_grad = (hidden_grad * up_pre * gate_slope).astype(BF16)
        up_grad = (hidden_grad * activated).astype(BF16)
        pre_grads[c] = (gate_grad, up_grad)
        weight_grad = jnp.sum(hidden.astype(F32) * raw_grad, axis=-1, keepdims=True)
        logits_grad = (sign * (slope * weight_grad)).astype(BF16)
        backs[c] = (
            dot(gate_grad, gate_mat, ((1,), (1,)))
            + dot(up_grad, up_mat, ((1,), (1,)))
            + dot(logits_grad, router[c, 0], ((1,), (1,)))
        ).astype(BF16)
        weighted_hidden = (hidden.astype(F32) * weight).astype(BF16)
        downs[c] = dot(weighted_hidden, upstream, ((0,), (0,)))
        routers[c] = dot(logits_grad, rows, ((0,), (0,)))

    next_fwd, prev_grad = {}, {}
    for c, way in ((1, -1), (0, 1)):
        inputs_wide = x_in[c, 0].astype(F32)
        section_out = (inputs_wide + scatter_rows(outs[c])).astype(BF16)
        next_fwd[c] = shifted(section_out, way)
        normed_grad = scatter_rows(backs[c])
        _, pullback = jax.vjp(lambda values: normalize(values, norm_gain[c, 0]), inputs_wide)
        input_grad = (out_grad[c, 0].astype(F32) + pullback(normed_grad)[0]).astype(BF16)
        prev_grad[c] = shifted(input_grad, -way)

    far_rows = gather_rows(mirrored(normed[1]))
    far_gate, far_up = mirrored(pre_grads[1][0]), mirrored(pre_grads[1][1])
    far_down = mirrored(downs[1].astype(BF16))

    def both(own, other):
        return (lax.reduce_precision(own, 8, 7) + lax.reduce_precision(other.astype(F32), 8, 7)).astype(BF16)

    grad_gate = both(dot(rows_all[0], pre_grads[0][0], ((0,), (0,))), dot(far_rows, far_gate, ((0,), (0,))))
    grad_up = both(dot(rows_all[0], pre_grads[0][1], ((0,), (0,))), dot(far_rows, far_up, ((0,), (0,))))
    grad_down = both(downs[0], far_down)
    router_sums = sum_small(jnp.concatenate([routers[0], routers[1]]))
    far_router = mirrored(router_sums[experts:].astype(BF16))
    grad_router = both(router_sums[:experts], far_router).T
    return (
        jnp.stack([next_fwd[0], next_fwd[1]])[:, None],
        jnp.stack([prev_grad[0], prev_grad[1]])[:, None],
        grad_gate[None],
        grad_up[None],
        grad_down[None],
        grad_router[None],
    )


def solution(mesh):
    in_specs = (
        P(None, "section", "fsdp", None),
        P(None, "section", "fsdp", None),
        P(None, "section", "fsdp", None),
        P(None, "section", None),
        P(None, "section", None, None),
        P(None, "section", None, "fsdp"),
        P(None, "section", None, "fsdp"),
        P(None, "section", "fsdp", None),
    )
    out_specs = (
        P(None, "section", "fsdp", None),
        P(None, "section", "fsdp", None),
        P("section", None, "fsdp"),
        P("section", None, "fsdp"),
        P("section", "fsdp", None),
        P("section", None, None),
    )
    return jax.shard_map(
        on_device, mesh=mesh, in_specs=in_specs, out_specs=out_specs, check_vma=False
    )
```

time: 753 us -> 469 us (0.62)
  the two profiles are of different devices: /device:TPU:6 before, /device:TPU:1 now
where the time goes in v1:
time: 469 us; the launch traced here: 460 us
  waiting for transfers between devices  256 us (55%)
  starting transfers between devices  94.7 us (20%)
  matrix products  48.3 us (10%)
  local copies, waits for them, and re-layouts  31.5 us (7%)
  other arithmetic  27 us (6%)
    ppermute x60, waiting for transfers between devices, permuted(): return lax.ppermute(value, axis, pairs)  256 us
    ppermute x60, starting transfers between devices, permuted(): return lax.ppermute(value, axis, pairs)  94.7 us
    dot_general x24, matrix products, dot(): lax.dot_general(first, second, (contract, ((), ())), preferred_element_ty...  48.3 us
    unnamed x130, local copies, waits for them, and re-layouts  13.9 us
  transfers between devices with their start and end apart: 60, of which 33 were waited for; matrix products, arithmetic and copies ran while one was open for 21% of the time, Pallas kernels for 0%

profile of v1, /device:TPU:1, one launch (start us, length us, event | category | flops | bytes accessed | tf_op | source)
XLA Modules:
  0.0 460.2 jit_solution(6773268108607342959)
XLA Ops:
  3.5 2.3 constant_dynamic-update-slice_fusion.5
  5.7 2.5 collective-permute-start.14
  8.2 6.3 %collective-permute-start.47 = (bf16[64,3072]{1,0:T(8,128)(2,1)}, bf16[64,3072]{1,0:T(8,128)(2,1)}, u32[]{:S(2)}, u32[]{:S(2)}) collective-permute-start(bf16[64,3072]{1,0:T(8,128)(2,1)} %get-tuple-element.85), channel_id=1, source_target_pairs={{0,120},{8,112},{16,104},{24,96},{32,88},{40,80},{48,72},{56,64},{... | collective-permute-start | bytes 1179656 | tf_op jit(solution)/shard_map/ppermute | solution.py:14
  20.0 5.9 %collective-permute-done.5 = f32[2,12,64]{2,0,1:T(2,128)} collective-permute-done((f32[2,12,64]{2,0,1:T(2,128)}, f32[2,12,64]{2,0,1:T(2,128)}, u32[]{:S(2)}, u32[]{:S(2)}) %collective-permute-start.5) | collective-permute-done | bytes 6176 | tf_op jit(solution)/shard_map/ppermute | solution.py:14
  31.4 2.9 collective-permute-start.7
  54.1 1.8 constant_dynamic-update-slice_fusion.27
  55.9 2.5 collective-permute-start.38
  58.4 1.8 constant_dynamic-update-slice_fusion.30
  63.5 3.8 collective-permute-done.48
  68.1 2.7 collective-permute-start.2
  71.0 10.0 %collective-permute-done.37 = bf16[128,3072]{1,0:T(8,128)(2,1)S(1)} collective-permute-done((bf16[128,3072]{1,0:T(8,128)(2,1)S(1)}, bf16[128,3072]{1,0:T(8,128)(2,1)S(1)}, u32[]{:S(2)}, u32[]{:S(2)}) %collective-permute-start.37) | collective-permute-done | bytes 786464 | tf_op jit(solution)/shard_map/ppermute | solution.py:14
  82.6 15.2 %collective-permute-done.1 = bf16[128,3072]{1,0:T(8,128)(2,1)S(1)} collective-permute-done((bf16[128,3072]{1,0:T(8,128)(2,1)S(1)}, bf16[128,3072]{1,0:T(8,128)(2,1)S(1)}, u32[]{:S(2)}, u32[]{:S(2)}) %collective-permute-start.1) | collective-permute-done | bytes 786464 | tf_op jit(solution)/shard_map/ppermute | solution.py:14
  99.6 15.1 %collective-permute-done.26 = bf16[128,3072]{1,0:T(8,128)(2,1)S(1)} collective-permute-done((bf16[128,3072]{1,0:T(8,128)(2,1)S(1)}, bf16[128,3072]{1,0:T(8,128)(2,1)S(1)}, u32[]{:S(2)}, u32[]{:S(2)}) %collective-permute-start.26) | collective-permute-done | bytes 786464 | tf_op jit(solution)/shard_map/ppermute | solution.py:14
  116.6 23.5 %collective-permute-done.17 = bf16[64,3072]{1,0:T(8,128)(2,1)S(1)} collective-permute-done((bf16[64,3072]{1,0:T(8,128)(2,1)S(1)}, bf16[64,3072]{1,0:T(8,128)(2,1)S(1)}, u32[]{:S(2)}, u32[]{:S(2)}) %collective-permute-start.17) | collective-permute-done | bytes 393248 | tf_op jit(solution)/shard_map/ppermute | solution.py:14
  140.1 3.0 collective-permute-start.4
  145.4 2.3 fusion.8
  147.7 9.1 %collective-permute-done.3 = bf16[64,3072]{1,0:T(8,128)(2,1)S(1)} collective-permute-done((bf16[64,3072]{1,0:T(8,128)(2,1)S(1)}, bf16[64,3072]{1,0:T(8,128)(2,1)S(1)}, u32[]{:S(2)}, u32[]{:S(2)}) %collective-permute-start.3) | collective-permute-done | bytes 393248 | tf_op jit(solution)/shard_map/ppermute | solution.py:14
  156.9 2.7 collective-permute-start.29
  162.5 3.6 collective-permute-done.28
  171.0 1.8 multiply_convert_fusion.1
  172.8 4.4 collective-permute-done.40
  177.3 2.5 fusion.58
  179.8 10.9 %collective-permute-start.53 = (bf16[512,384]{0,1:T(8,128)(2,1)}, bf16[512,384]{0,1:T(8,128)(2,1)}, u32[]{:S(2)}, u32[]{:S(2)}) collective-permute-start(bf16[512,384]{0,1:T(8,128)(2,1)} %get-tuple-element.77), channel_id=1, source_target_pairs={{0,120},{8,112},{16,104},{24,96},{32,88},{40,80},{48,72},{56,64},{... | collective-permute-start | bytes 1179656 | tf_op jit(solution)/shard_map/ppermute | solution.py:14
  190.7 2.9 fusion.10
  193.6 1.9 fusion.129
  195.5 1.9 fusion.17
  200.1 3.5 multiply_convert_fusion
  205.8 1.9 fusion.6
  207.7 3.5 add_convert_fusion
  211.2 2.5 fusion.123
  213.8 3.5 fusion.21
  218.5 1.8 fusion.128
  222.3 2.8 convolution_convert_fusion
  227.8 3.2 collective-permute-start.58
  232.3 9.7 %collective-permute-done.58 = f32[8,3072]{1,0:T(8,128)S(1)} collective-permute-done((f32[8,3072]{1,0:T(8,128)S(1)}, f32[8,3072]{1,0:T(8,128)S(1)}, u32[]{:S(2)}, u32[]{:S(2)}) %collective-permute-start.58) | collective-permute-done | bytes 98336 | tf_op jit(solution)/shard_map/ppermute | solution.py:14
  245.4 3.9 collective-permute-done.59
  249.3 1.9 collective-permute-start.8
  252.6 8.2 %collective-permute-done.8 = bf16[64,3072]{1,0:T(8,128)(2,1)S(1)} collective-permute-done((bf16[64,3072]{1,0:T(8,128)(2,1)S(1)}, bf16[64,3072]{1,0:T(8,128)(2,1)S(1)}, u32[]{:S(2)}, u32[]{:S(2)}) %collective-permute-start.8) | collective-permute-done | bytes 393248 | tf_op jit(solution)/shard_map/ppermute | solution.py:14
  261.0 8.2 %collective-permute-done.19 = bf16[64,3072]{1,0:T(8,128)(2,1)S(1)} collective-permute-done((bf16[64,3072]{1,0:T(8,128)(2,1)S(1)}, bf16[64,3072]{1,0:T(8,128)(2,1)S(1)}, u32[]{:S(2)}, u32[]{:S(2)}) %collective-permute-start.19) | collective-permute-done | bytes 393248 | tf_op jit(solution)/shard_map/ppermute | solution.py:14
  269.9 2.1 collective-permute-start.43
  272.1 7.8 %collective-permute-done.41 = bf16[64,3072]{1,0:T(8,128)(2,1)S(1)} collective-permute-done((bf16[64,3072]{1,0:T(8,128)(2,1)S(1)}, bf16[64,3072]{1,0:T(8,128)(2,1)S(1)}, u32[]{:S(2)}, u32[]{:S(2)}) %collective-permute-start.41) | collective-permute-done | bytes 393248 | tf_op jit(solution)/shard_map/ppermute | solution.py:14
  279.9 2.7 collective-permute-start.32
  282.9 6.7 %collective-permute-done.30 = bf16[64,3072]{1,0:T(8,128)(2,1)S(1)} collective-permute-done((bf16[64,3072]{1,0:T(8,128)(2,1)S(1)}, bf16[64,3072]{1,0:T(8,128)(2,1)S(1)}, u32[]{:S(2)}, u32[]{:S(2)}) %collective-permute-start.30) | collective-permute-done | bytes 393248 | tf_op jit(solution)/shard_map/ppermute | solution.py:14
  292.8 5.2 %collective-permute-done.52 = bf16[64,3072]{1,0:T(8,128)(2,1)S(1)} collective-permute-done((bf16[64,3072]{1,0:T(8,128)(2,1)S(1)}, bf16[64,3072]{1,0:T(8,128)(2,1)S(1)}, u32[]{:S(2)}, u32[]{:S(2)}) %collective-permute-start.52) | collective-permute-done | bytes 393248 | tf_op jit(solution)/shard_map/ppermute | solution.py:14
  298.2 3.5 collective-permute-start.44
  301.7 3.4 fusion.1
  306.9 8.0 %collective-permute-done.22 = bf16[128,3072]{1,0:T(8,128)(2,1)} collective-permute-done((bf16[128,3072]{1,0:T(8,128)(2,1)S(1)}, bf16[128,3072]{1,0:T(8,128)(2,1)}, u32[]{:S(2)}, u32[]{:S(2)}) %collective-permute-start.22) | collective-permute-done | bytes 786464 | tf_op jit(solution)/shard_map/ppermute | solution.py:14
  314.9 3.5 collective-permute-start.33
  319.9 2.8 collective-permute-done.42
  323.8 8.0 %collective-permute-done.44 = bf16[128,3072]{1,0:T(8,128)(2,1)} collective-permute-done((bf16[128,3072]{1,0:T(8,128)(2,1)S(1)}, bf16[128,3072]{1,0:T(8,128)(2,1)}, u32[]{:S(2)}, u32[]{:S(2)}) %collective-permute-start.44) | collective-permute-done | bytes 786464 | tf_op jit(solution)/shard_map/ppermute | solution.py:14
  331.8 3.5 collective-permute-start.11
  336.8 2.7 collective-permute-done.31
  339.5 10.6 %collective-permute-start.55 = (bf16[384,3072]{1,0:T(8,128)(2,1)S(1)}, bf16[384,3072]{1,0:T(8,128)(2,1)S(1)}, u32[]{:S(2)}, u32[]{:S(2)}) collective-permute-start(bf16[384,3072]{1,0:T(8,128)(2,1)S(1)} %copy-done.44), channel_id=1, source_target_pairs={{0,120},{8,112},{16,104},{24,96},{32,88},{40,80},{48,72},{56,64},{... | collective-permute-start | bytes 7077896 | tf_op jit(solution)/shard_map/ppermute | solution.py:14
  350.5 5.9 %collective-permute-done.9 = bf16[128,3072]{1,0:T(8,128)(2,1)S(1)} collective-permute-done((bf16[128,3072]{1,0:T(8,128)(2,1)S(1)}, bf16[128,3072]{1,0:T(8,128)(2,1)S(1)}, u32[]{:S(2)}, u32[]{:S(2)}) %collective-permute-start.9) | collective-permute-done | bytes 786464 | tf_op jit(solution)/shard_map/ppermute | solution.py:14
  357.7 7.8 %collective-permute-done.11 = bf16[128,3072]{1,0:T(8,128)(2,1)S(1)} collective-permute-done((bf16[128,3072]{1,0:T(8,128)(2,1)S(1)}, bf16[128,3072]{1,0:T(8,128)(2,1)S(1)}, u32[]{:S(2)}, u32[]{:S(2)}) %collective-permute-start.11) | collective-permute-done | bytes 786464 | tf_op jit(solution)/shard_map/ppermute | solution.py:14
  367.0 42.0 %collective-permute-done.23 = bf16[64,3072]{1,0:T(8,128)(2,1)S(1)} collective-permute-done((bf16[64,3072]{1,0:T(8,128)(2,1)S(1)}, bf16[64,3072]{1,0:T(8,128)(2,1)S(1)}, u32[]{:S(2)}, u32[]{:S(2)}) %collective-permute-start.23) | collective-permute-done | bytes 393248 | tf_op jit(solution)/shard_map/ppermute | solution.py:14
  410.6 6.9 %collective-permute-done.45 = bf16[64,3072]{1,0:T(8,128)(2,1)S(1)} collective-permute-done((bf16[64,3072]{1,0:T(8,128)(2,1)S(1)}, bf16[64,3072]{1,0:T(8,128)(2,1)S(1)}, u32[]{:S(2)}, u32[]{:S(2)}) %collective-permute-start.45) | collective-permute-done | bytes 393248 | tf_op jit(solution)/shard_map/ppermute | solution.py:14
  417.5 8.4 %collective-permute-done.34 = bf16[64,3072]{1,0:T(8,128)(2,1)S(1)} collective-permute-done((bf16[64,3072]{1,0:T(8,128)(2,1)S(1)}, bf16[64,3072]{1,0:T(8,128)(2,1)S(1)}, u32[]{:S(2)}, u32[]{:S(2)}) %collective-permute-start.34) | collective-permute-done | bytes 393248 | tf_op jit(solution)/shard_map/ppermute | solution.py:14
  426.5 7.8 %collective-permute-done.12 = bf16[64,3072]{1,0:T(8,128)(2,1)S(1)} collective-permute-done((bf16[64,3072]{1,0:T(8,128)(2,1)S(1)}, bf16[64,3072]{1,0:T(8,128)(2,1)S(1)}, u32[]{:S(2)}, u32[]{:S(2)}) %collective-permute-start.12) | collective-permute-done | bytes 393248 | tf_op jit(solution)/shard_map/ppermute | solution.py:14
  435.7 2.8 collective-permute-start.46
  439.0 4.3 fusion
  443.3 9.0 %collective-permute-done.35 = bf16[64,3072]{1,0:T(8,128)(2,1)S(1)} collective-permute-done((bf16[64,3072]{1,0:T(8,128)(2,1)S(1)}, bf16[64,3072]{1,0:T(8,128)(2,1)S(1)}, u32[]{:S(2)}, u32[]{:S(2)}) %collective-permute-start.35) | collective-permute-done | bytes 393248 | tf_op jit(solution)/shard_map/ppermute | solution.py:14
  453.3 2.5 collective-permute-done.13
  457.5 2.2 fusion.2
  (304 shorter events, 89.7 us)
Async XLA Ops:
  5.7 41.9 %collective-permute-start.14 = (bf16[64,3072]{1,0:T(8,128)(2,1)}, bf16[64,3072]{1,0:T(8,128)(2,1)S(1)}, u32[]{:S(2)}, u32[]{:S(2)}) collective-permute-start(bf16[64,3072]{1,0:T(8,128)(2,1)} %get-tuple-element.85), channel_id=1, source_target_pairs={{0,4},{1,5},{2,6},{3,7},{4,0},{5,1},{6,2},{7,3},{8,12},{9,13},{10,... | collective-permute-start | bytes 1179656 | tf_op jit(solution)/shard_map/ppermute | solution.py:14
  8.2 47.6 %collective-permute-start.47 = (bf16[64,3072]{1,0:T(8,128)(2,1)}, bf16[64,3072]{1,0:T(8,128)(2,1)}, u32[]{:S(2)}, u32[]{:S(2)}) collective-permute-start(bf16[64,3072]{1,0:T(8,128)(2,1)} %get-tuple-element.85), channel_id=1, source_target_pairs={{0,120},{8,112},{16,104},{24,96},{32,88},{40,80},{48,72},{56,64},{... | collective-permute-start | bytes 1179656 | tf_op jit(solution)/shard_map/ppermute | solution.py:14
  16.0 10.0 %collective-permute-start.5 = (f32[2,12,64]{2,0,1:T(2,128)}, f32[2,12,64]{2,0,1:T(2,128)}, u32[]{:S(2)}, u32[]{:S(2)}) collective-permute-start(f32[2,12,64]{2,0,1:T(2,128)} %get-tuple-element.101), channel_id=1, source_target_pairs={{0,4},{1,5},{2,6},{3,7},{4,0},{5,1},{6,2},{7,3},{8,12},{9,13},{10,... | collective-permute-start | bytes 18440 | tf_op jit(solution)/shard_map/ppermute | solution.py:14
  16.9 32.9 %collective-permute-start.36 = (bf16[64,3072]{1,0:T(8,128)(2,1)}, bf16[64,3072]{1,0:T(8,128)(2,1)}, u32[]{:S(2)}, u32[]{:S(2)}) collective-permute-start(bf16[64,3072]{1,0:T(8,128)(2,1)} %get-tuple-element.87), channel_id=1, source_target_pairs={{0,4},{1,5},{2,6},{3,7},{4,0},{5,1},{6,2},{7,3},{8,12},{9,13},{10,... | collective-permute-start | bytes 1179656 | tf_op jit(solution)/shard_map/ppermute | solution.py:14
  18.4 34.3 %collective-permute-start = (bf16[64,3072]{1,0:T(8,128)(2,1)}, bf16[64,3072]{1,0:T(8,128)(2,1)}, u32[]{:S(2)}, u32[]{:S(2)}) collective-permute-start(bf16[64,3072]{1,0:T(8,128)(2,1)} %get-tuple-element.45), channel_id=1, source_target_pairs={{0,4},{1,5},{2,6},{3,7},{4,0},{5,1},{6,2},{7,3},{8,12},{9,13},{10,... | collective-permute-start | bytes 1179656 | tf_op jit(solution)/shard_map/ppermute | solution.py:14
  27.3 3.3 collective-permute-start.6
  31.4 4.6 collective-permute-start.7
  35.9 24.2 %collective-permute-start.25 = (bf16[64,3072]{1,0:T(8,128)(2,1)}, bf16[64,3072]{1,0:T(8,128)(2,1)}, u32[]{:S(2)}, u32[]{:S(2)}) collective-permute-start(bf16[64,3072]{1,0:T(8,128)(2,1)} %get-tuple-element.86), channel_id=1, source_target_pairs={{0,4},{1,5},{2,6},{3,7},{4,0},{5,1},{6,2},{7,3},{8,12},{9,13},{10,... | collective-permute-start | bytes 1179656 | tf_op jit(solution)/shard_map/ppermute | solution.py:14
  47.6 129.7 %copy-start.42 = (f32[512]{0:T(512)}, f32[512]{0:T(512)S(1)}, u32[]{:S(2)}) copy-start(f32[512]{0:T(512)S(1)} %get-tuple-element.38) | copy-start | bytes 6148
  48.7 19.4 %collective-permute-start.15 = (bf16[128,3072]{1,0:T(8,128)(2,1)S(1)}, bf16[128,3072]{1,0:T(8,128)(2,1)S(1)}, u32[]{:S(2)}, u32[]{:S(2)}) collective-permute-start(bf16[128,3072]{1,0:T(8,128)(2,1)S(1)} %pad_maximum_fusion.3), channel_id=1, source_target_pairs={{0,1},{1,2},{2,3},{3,0},{4,5},{5,6},{6,7},{7,4},{8,9},{9,10},{10,1... | collective-permute-start | bytes 2359304 | tf_op jit(solution)/shard_map/ppermute | solution.py:14
  49.8 21.1 %collective-permute-start.16 = (bf16[128,3072]{1,0:T(8,128)(2,1)S(1)}, bf16[128,3072]{1,0:T(8,128)(2,1)S(1)}, u32[]{:S(2)}, u32[]{:S(2)}) collective-permute-start(bf16[128,3072]{1,0:T(8,128)(2,1)S(1)} %pad_maximum_fusion.3), channel_id=1, source_target_pairs={{0,3},{1,0},{2,1},{3,2},{4,7},{5,4},{6,5},{7,6},{8,11},{9,8},{10,9... | collective-permute-start | bytes 2359304 | tf_op jit(solution)/shard_map/ppermute | solution.py:14
  52.6 28.4 %collective-permute-start.37 = (bf16[128,3072]{1,0:T(8,128)(2,1)S(1)}, bf16[128,3072]{1,0:T(8,128)(2,1)S(1)}, u32[]{:S(2)}, u32[]{:S(2)}) collective-permute-start(bf16[128,3072]{1,0:T(8,128)(2,1)S(1)} %pad_maximum_fusion.9), channel_id=1, source_target_pairs={{0,1},{1,2},{2,3},{3,0},{4,5},{5,6},{6,7},{7,4},{8,9},{9,10},{10,1... | collective-permute-start | bytes 2359304 | tf_op jit(solution)/shard_map/ppermute | solution.py:14
  55.9 26.0 %collective-permute-start.38 = (bf16[128,3072]{1,0:T(8,128)(2,1)S(1)}, bf16[128,3072]{1,0:T(8,128)(2,1)S(1)}, u32[]{:S(2)}, u32[]{:S(2)}) collective-permute-start(bf16[128,3072]{1,0:T(8,128)(2,1)S(1)} %pad_maximum_fusion.9), channel_id=1, source_target_pairs={{0,3},{1,0},{2,1},{3,2},{4,7},{5,4},{6,5},{7,6},{8,11},{9,8},{10,9... | collective-permute-start | bytes 2359304 | tf_op jit(solution)/shard_map/ppermute | solution.py:14
  60.2 7.1 %collective-permute-start.48 = (bf16[64,3072]{1,0:T(8,128)(2,1)}, bf16[64,3072]{1,0:T(8,128)(2,1)S(1)}, u32[]{:S(2)}, u32[]{:S(2)}) collective-permute-start(bf16[64,3072]{1,0:T(8,128)(2,1)} %collective-permute-done.47), channel_id=1, source_target_pairs={{0,4},{1,5},{2,6},{3,7},{4,0},{5,1},{6,2},{7,3},{8,12},{9,13},{10,... | collective-permute-start | bytes 1179656 | tf_op jit(solution)/shard_map/ppermute | solution.py:14
  67.3 30.5 %collective-permute-start.1 = (bf16[128,3072]{1,0:T(8,128)(2,1)S(1)}, bf16[128,3072]{1,0:T(8,128)(2,1)S(1)}, u32[]{:S(2)}, u32[]{:S(2)}) collective-permute-start(bf16[128,3072]{1,0:T(8,128)(2,1)S(1)} %pad_maximum_fusion), channel_id=1, source_target_pairs={{0,1},{1,2},{2,3},{3,0},{4,5},{5,6},{6,7},{7,4},{8,9},{9,10},{10,1... | collective-permute-start | bytes 2359304 | tf_op jit(solution)/shard_map/ppermute | solution.py:14
  68.1 30.6 %collective-permute-start.2 = (bf16[128,3072]{1,0:T(8,128)(2,1)S(1)}, bf16[128,3072]{1,0:T(8,128)(2,1)S(1)}, u32[]{:S(2)}, u32[]{:S(2)}) collective-permute-start(bf16[128,3072]{1,0:T(8,128)(2,1)S(1)} %pad_maximum_fusion), channel_id=1, source_target_pairs={{0,3},{1,0},{2,1},{3,2},{4,7},{5,4},{6,5},{7,6},{8,11},{9,8},{10,9... | collective-permute-start | bytes 2359304 | tf_op jit(solution)/shard_map/ppermute | solution.py:14
  70.8 43.8 %collective-permute-start.26 = (bf16[128,3072]{1,0:T(8,128)(2,1)S(1)}, bf16[128,3072]{1,0:T(8,128)(2,1)S(1)}, u32[]{:S(2)}, u32[]{:S(2)}) collective-permute-start(bf16[128,3072]{1,0:T(8,128)(2,1)S(1)} %pad_maximum_fusion.6), channel_id=1, source_target_pairs={{0,1},{1,2},{2,3},{3,0},{4,5},{5,6},{6,7},{7,4},{8,9},{9,10},{10,1... | collective-permute-start | bytes 2359304 | tf_op jit(solution)/shard_map/ppermute | solution.py:14
  81.0 34.6 %collective-permute-start.27 = (bf16[128,3072]{1,0:T(8,128)(2,1)S(1)}, bf16[128,3072]{1,0:T(8,128)(2,1)S(1)}, u32[]{:S(2)}, u32[]{:S(2)}) collective-permute-start(bf16[128,3072]{1,0:T(8,128)(2,1)S(1)} %pad_maximum_fusion.6), channel_id=1, source_target_pairs={{0,3},{1,0},{2,1},{3,2},{4,7},{5,4},{6,5},{7,6},{8,11},{9,8},{10,9... | collective-permute-start | bytes 2359304 | tf_op jit(solution)/shard_map/ppermute | solution.py:14
  81.8 144.3 %collective-permute-start.49 = (bf16[128,3072]{1,0:T(8,128)(2,1)}, bf16[128,3072]{1,0:T(8,128)(2,1)}, u32[]{:S(2)}, u32[]{:S(2)}) collective-permute-start(bf16[128,3072]{1,0:T(8,128)(2,1)} %get-tuple-element.90), channel_id=1, source_target_pairs={{0,1},{1,2},{2,3},{3,0},{4,5},{5,6},{6,7},{7,4},{8,9},{9,10},{10,1... | collective-permute-start | bytes 2359304 | tf_op jit(solution)/shard_map/ppermute | solution.py:14
  97.8 144.5 %collective-permute-start.50 = (bf16[128,3072]{1,0:T(8,128)(2,1)}, bf16[128,3072]{1,0:T(8,128)(2,1)}, u32[]{:S(2)}, u32[]{:S(2)}) collective-permute-start(bf16[128,3072]{1,0:T(8,128)(2,1)} %get-tuple-element.90), channel_id=1, source_target_pairs={{0,3},{1,0},{2,1},{3,2},{4,7},{5,4},{6,5},{7,6},{8,11},{9,8},{10,9... | collective-permute-start | bytes 2359304 | tf_op jit(solution)/shard_map/ppermute | solution.py:14
  98.8 41.3 %collective-permute-start.17 = (bf16[64,3072]{1,0:T(8,128)(2,1)S(1)}, bf16[64,3072]{1,0:T(8,128)(2,1)S(1)}, u32[]{:S(2)}, u32[]{:S(2)}) collective-permute-start(bf16[64,3072]{1,0:T(8,128)(2,1)S(1)} %slice.377), channel_id=1, source_target_pairs={{0,1},{1,2},{2,3},{3,0},{4,5},{5,6},{6,7},{7,4},{8,9},{9,10},{10,1... | collective-permute-start | bytes 1179656 | tf_op jit(solution)/shard_map/ppermute | solution.py:14
  114.7 25.4 %collective-permute-start.18 = (bf16[64,3072]{1,0:T(8,128)(2,1)S(1)}, bf16[64,3072]{1,0:T(8,128)(2,1)S(1)}, u32[]{:S(2)}, u32[]{:S(2)}) collective-permute-start(bf16[64,3072]{1,0:T(8,128)(2,1)S(1)} %slice.378), channel_id=1, source_target_pairs={{0,3},{1,0},{2,1},{3,2},{4,7},{5,4},{6,5},{7,6},{8,11},{9,8},{10,9... | collective-permute-start | bytes 1179656 | tf_op jit(solution)/shard_map/ppermute | solution.py:14
  115.6 55.3 %collective-permute-start.39 = (bf16[64,3072]{1,0:T(8,128)(2,1)S(1)}, bf16[64,3072]{1,0:T(8,128)(2,1)S(1)}, u32[]{:S(2)}, u32[]{:S(2)}) collective-permute-start(bf16[64,3072]{1,0:T(8,128)(2,1)S(1)} %slice.403), channel_id=1, source_target_pairs={{0,1},{1,2},{2,3},{3,0},{4,5},{5,6},{6,7},{7,4},{8,9},{9,10},{10,1... | collective-permute-start | bytes 1179656 | tf_op jit(solution)/shard_map/ppermute | solution.py:14
  140.1 16.7 %collective-permute-start.3 = (bf16[64,3072]{1,0:T(8,128)(2,1)S(1)}, bf16[64,3072]{1,0:T(8,128)(2,1)S(1)}, u32[]{:S(2)}, u32[]{:S(2)}) collective-permute-start(bf16[64,3072]{1,0:T(8,128)(2,1)S(1)} %slice.362), channel_id=1, source_target_pairs={{0,1},{1,2},{2,3},{3,0},{4,5},{5,6},{6,7},{7,4},{8,9},{9,10},{10,1... | collective-permute-start | bytes 1179656 | tf_op jit(solution)/shard_map/ppermute | solution.py:14
  140.1 16.7 %collective-permute-start.4 = (bf16[64,3072]{1,0:T(8,128)(2,1)S(1)}, bf16[64,3072]{1,0:T(8,128)(2,1)S(1)}, u32[]{:S(2)}, u32[]{:S(2)}) collective-permute-start(bf16[64,3072]{1,0:T(8,128)(2,1)S(1)} %slice.363), channel_id=1, source_target_pairs={{0,3},{1,0},{2,1},{3,2},{4,7},{5,4},{6,5},{7,6},{8,11},{9,8},{10,9... | collective-permute-start | bytes 1179656 | tf_op jit(solution)/shard_map/ppermute | solution.py:14
  156.8 9.3 %collective-permute-start.28 = (bf16[64,3072]{1,0:T(8,128)(2,1)S(1)}, bf16[64,3072]{1,0:T(8,128)(2,1)S(1)}, u32[]{:S(2)}, u32[]{:S(2)}) collective-permute-start(bf16[64,3072]{1,0:T(8,128)(2,1)S(1)} %slice.390), channel_id=1, source_target_pairs={{0,1},{1,2},{2,3},{3,0},{4,5},{5,6},{6,7},{7,4},{8,9},{9,10},{10,1... | collective-permute-start | bytes 1179656 | tf_op jit(solution)/shard_map/ppermute | solution.py:14
  156.9 10.8 %collective-permute-start.29 = (bf16[64,3072]{1,0:T(8,128)(2,1)S(1)}, bf16[64,3072]{1,0:T(8,128)(2,1)S(1)}, u32[]{:S(2)}, u32[]{:S(2)}) collective-permute-start(bf16[64,3072]{1,0:T(8,128)(2,1)S(1)} %slice.391), channel_id=1, source_target_pairs={{0,3},{1,0},{2,1},{3,2},{4,7},{5,4},{6,5},{7,6},{8,11},{9,8},{10,9... | collective-permute-start | bytes 1179656 | tf_op jit(solution)/shard_map/ppermute | solution.py:14
  166.1 11.1 %collective-permute-start.40 = (bf16[64,3072]{1,0:T(8,128)(2,1)S(1)}, bf16[64,3072]{1,0:T(8,128)(2,1)S(1)}, u32[]{:S(2)}, u32[]{:S(2)}) collective-permute-start(bf16[64,3072]{1,0:T(8,128)(2,1)S(1)} %slice.404), channel_id=1, source_target_pairs={{0,3},{1,0},{2,1},{3,2},{4,7},{5,4},{6,5},{7,6},{8,11},{9,8},{10,9... | collective-permute-start | bytes 1179656 | tf_op jit(solution)/shard_map/ppermute | solution.py:14
  179.8 258.7 %collective-permute-start.53 = (bf16[512,384]{0,1:T(8,128)(2,1)}, bf16[512,384]{0,1:T(8,128)(2,1)}, u32[]{:S(2)}, u32[]{:S(2)}) collective-permute-start(bf16[512,384]{0,1:T(8,128)(2,1)} %get-tuple-element.77), channel_id=1, source_target_pairs={{0,120},{8,112},{16,104},{24,96},{32,88},{40,80},{48,72},{56,64},{... | collective-permute-start | bytes 1179656 | tf_op jit(solution)/shard_map/ppermute | solution.py:14
  198.7 21.7 %collective-permute-start.56 = (f32[8,3072]{1,0:T(8,128)S(1)}, f32[8,3072]{1,0:T(8,128)}, u32[]{:S(2)}, u32[]{:S(2)}) collective-permute-start(f32[8,3072]{1,0:T(8,128)S(1)} %pad_maximum_fusion.12), channel_id=1, source_target_pairs={{0,4},{1,5},{2,6},{3,7},{4,0},{5,1},{6,2},{7,3},{8,12},{9,13},{10,... | collective-permute-start | bytes 294920 | tf_op jit(solution)/shard_map/ppermute | solution.py:14
  221.3 6.4 %collective-permute-start.57 = (f32[8,3072]{1,0:T(8,128)S(1)}, f32[8,3072]{1,0:T(8,128)S(1)}, u32[]{:S(2)}, u32[]{:S(2)}) collective-permute-start(f32[8,3072]{1,0:T(8,128)S(1)} %fusion.119), channel_id=1, source_target_pairs={{0,1},{1,0},{2,3},{3,2},{4,5},{5,4},{6,7},{7,6},{8,9},{9,8},{10,11... | collective-permute-start | bytes 294920 | tf_op jit(solution)/shard_map/ppermute | solution.py:14
  225.2 73.0 %collective-permute-start.54 = (bf16[512,384]{0,1:T(8,128)(2,1)S(1)}, bf16[512,384]{0,1:T(8,128)(2,1)S(1)}, u32[]{:S(2)}, u32[]{:S(2)}) collective-permute-start(bf16[512,384]{0,1:T(8,128)(2,1)S(1)} %copy-done.19), channel_id=1, source_target_pairs={{0,120},{8,112},{16,104},{24,96},{32,88},{40,80},{48,72},{56,64},{... | collective-permute-start | bytes 1179656 | tf_op jit(solution)/shard_map/ppermute | solution.py:14
  227.2 64.3 %collective-permute-start.51 = (bf16[64,3072]{1,0:T(8,128)(2,1)S(1)}, bf16[64,3072]{1,0:T(8,128)(2,1)S(1)}, u32[]{:S(2)}, u32[]{:S(2)}) collective-permute-start(bf16[64,3072]{1,0:T(8,128)(2,1)S(1)} %slice.416), channel_id=1, source_target_pairs={{0,1},{1,2},{2,3},{3,0},{4,5},{5,6},{6,7},{7,4},{8,9},{9,10},{10,1... | collective-permute-start | bytes 1179656 | tf_op jit(solution)/shard_map/ppermute | solution.py:14
  227.8 14.3 %collective-permute-start.58 = (f32[8,3072]{1,0:T(8,128)S(1)}, f32[8,3072]{1,0:T(8,128)S(1)}, u32[]{:S(2)}, u32[]{:S(2)}) collective-permute-start(f32[8,3072]{1,0:T(8,128)S(1)} %add.223), channel_id=1, source_target_pairs={{0,2},{1,3},{2,0},{3,1},{4,6},{5,7},{6,4},{7,5},{8,10},{9,11},{10,... | collective-permute-start | bytes 294920 | tf_op jit(solution)/shard_map/ppermute | solution.py:14
  242.0 10.5 %collective-permute-start.10 = (bf16[64,3072]{1,0:T(8,128)(2,1)S(1)}, bf16[64,3072]{1,0:T(8,128)(2,1)S(1)}, u32[]{:S(2)}, u32[]{:S(2)}) collective-permute-start(bf16[64,3072]{1,0:T(8,128)(2,1)S(1)} %copy-done.25), channel_id=1, source_target_pairs={{0,3},{1,0},{2,1},{3,2},{4,7},{5,4},{6,5},{7,6},{8,11},{9,8},{10,9... | collective-permute-start | bytes 1179656 | tf_op jit(solution)/shard_map/ppermute | solution.py:14
  242.3 6.9 %collective-permute-start.59 = (bf16[4,3072]{1,0:T(4,128)(2,1)S(1)}, bf16[4,3072]{1,0:T(4,128)(2,1)S(1)}, u32[]{:S(2)}, u32[]{:S(2)}) collective-permute-start(bf16[4,3072]{1,0:T(4,128)(2,1)S(1)} %slice.596), channel_id=1, source_target_pairs={{0,120},{8,112},{16,104},{24,96},{32,88},{40,80},{48,72},{56,64},{... | collective-permute-start | bytes 73736 | tf_op jit(solution)/shard_map/ppermute | solution.py:14
  249.3 11.6 %collective-permute-start.8 = (bf16[64,3072]{1,0:T(8,128)(2,1)S(1)}, bf16[64,3072]{1,0:T(8,128)(2,1)S(1)}, u32[]{:S(2)}, u32[]{:S(2)}) collective-permute-start(bf16[64,3072]{1,0:T(8,128)(2,1)S(1)} %copy-done.24), channel_id=1, source_target_pairs={{0,1},{1,2},{2,3},{3,0},{4,5},{5,6},{6,7},{7,4},{8,9},{9,10},{10,1... | collective-permute-start | bytes 1179656 | tf_op jit(solution)/shard_map/ppermute | solution.py:14
  252.6 16.7 %collective-permute-start.19 = (bf16[64,3072]{1,0:T(8,128)(2,1)S(1)}, bf16[64,3072]{1,0:T(8,128)(2,1)S(1)}, u32[]{:S(2)}, u32[]{:S(2)}) collective-permute-start(bf16[64,3072]{1,0:T(8,128)(2,1)S(1)} %copy-done.23), channel_id=1, source_target_pairs={{0,1},{1,2},{2,3},{3,0},{4,5},{5,6},{6,7},{7,4},{8,9},{9,10},{10,1... | collective-permute-start | bytes 1179656 | tf_op jit(solution)/shard_map/ppermute | solution.py:14
  260.8 9.0 %collective-permute-start.21 = (bf16[64,3072]{1,0:T(8,128)(2,1)S(1)}, bf16[64,3072]{1,0:T(8,128)(2,1)S(1)}, u32[]{:S(2)}, u32[]{:S(2)}) collective-permute-start(bf16[64,3072]{1,0:T(8,128)(2,1)S(1)} %copy-done.22), channel_id=1, source_target_pairs={{0,3},{1,0},{2,1},{3,2},{4,7},{5,4},{6,5},{7,6},{8,11},{9,8},{10,9... | collective-permute-start | bytes 1179656 | tf_op jit(solution)/shard_map/ppermute | solution.py:14
  269.2 10.6 %collective-permute-start.41 = (bf16[64,3072]{1,0:T(8,128)(2,1)S(1)}, bf16[64,3072]{1,0:T(8,128)(2,1)S(1)}, u32[]{:S(2)}, u32[]{:S(2)}) collective-permute-start(bf16[64,3072]{1,0:T(8,128)(2,1)S(1)} %copy-done.21), channel_id=1, source_target_pairs={{0,1},{1,2},{2,3},{3,0},{4,5},{5,6},{6,7},{7,4},{8,9},{9,10},{10,1... | collective-permute-start | bytes 1179656 | tf_op jit(solution)/shard_map/ppermute | solution.py:14
  269.9 10.0 %collective-permute-start.43 = (bf16[64,3072]{1,0:T(8,128)(2,1)S(1)}, bf16[64,3072]{1,0:T(8,128)(2,1)S(1)}, u32[]{:S(2)}, u32[]{:S(2)}) collective-permute-start(bf16[64,3072]{1,0:T(8,128)(2,1)S(1)} %copy-done.20), channel_id=1, source_target_pairs={{0,3},{1,0},{2,1},{3,2},{4,7},{5,4},{6,5},{7,6},{8,11},{9,8},{10,9... | collective-permute-start | bytes 1179656 | tf_op jit(solution)/shard_map/ppermute | solution.py:14
  279.9 9.7 %collective-permute-start.30 = (bf16[64,3072]{1,0:T(8,128)(2,1)S(1)}, bf16[64,3072]{1,0:T(8,128)(2,1)S(1)}, u32[]{:S(2)}, u32[]{:S(2)}) collective-permute-start(bf16[64,3072]{1,0:T(8,128)(2,1)S(1)} %get-tuple-element.54), channel_id=1, source_target_pairs={{0,1},{1,2},{2,3},{3,0},{4,5},{5,6},{6,7},{7,4},{8,9},{9,10},{10,1... | collective-permute-start | bytes 1179656 | tf_op jit(solution)/shard_map/ppermute | solution.py:14
  279.9 9.7 %collective-permute-start.32 = (bf16[64,3072]{1,0:T(8,128)(2,1)S(1)}, bf16[64,3072]{1,0:T(8,128)(2,1)S(1)}, u32[]{:S(2)}, u32[]{:S(2)}) collective-permute-start(bf16[64,3072]{1,0:T(8,128)(2,1)S(1)} %get-tuple-element.55), channel_id=1, source_target_pairs={{0,3},{1,0},{2,1},{3,2},{4,7},{5,4},{6,5},{7,6},{8,11},{9,8},{10,9... | collective-permute-start | bytes 1179656 | tf_op jit(solution)/shard_map/ppermute | solution.py:14
  289.6 8.4 %collective-permute-start.52 = (bf16[64,3072]{1,0:T(8,128)(2,1)S(1)}, bf16[64,3072]{1,0:T(8,128)(2,1)S(1)}, u32[]{:S(2)}, u32[]{:S(2)}) collective-permute-start(bf16[64,3072]{1,0:T(8,128)(2,1)S(1)} %slice.417), channel_id=1, source_target_pairs={{0,3},{1,0},{2,1},{3,2},{4,7},{5,4},{6,5},{7,6},{8,11},{9,8},{10,9... | collective-permute-start | bytes 1179656 | tf_op jit(solution)/shard_map/ppermute | solution.py:14
  289.6 16.2 %collective-permute-start.20 = (bf16[128,3072]{1,0:T(8,128)(2,1)S(1)}, bf16[128,3072]{1,0:T(8,128)(2,1)S(1)}, u32[]{:S(2)}, u32[]{:S(2)}) collective-permute-start(bf16[128,3072]{1,0:T(8,128)(2,1)S(1)} %pad_maximum_fusion.4), channel_id=1, source_target_pairs={{0,1},{1,2},{2,3},{3,0},{4,5},{5,6},{6,7},{7,4},{8,9},{9,10},{10,1... | collective-permute-start | bytes 2359304 | tf_op jit(solution)/shard_map/ppermute | solution.py:14
  291.4 23.5 %collective-permute-start.22 = (bf16[128,3072]{1,0:T(8,128)(2,1)S(1)}, bf16[128,3072]{1,0:T(8,128)(2,1)}, u32[]{:S(2)}, u32[]{:S(2)}) collective-permute-start(bf16[128,3072]{1,0:T(8,128)(2,1)S(1)} %pad_maximum_fusion.5), channel_id=1, source_target_pairs={{0,3},{1,0},{2,1},{3,2},{4,7},{5,4},{6,5},{7,6},{8,11},{9,8},{10,9... | collective-permute-start | bytes 2359304 | tf_op jit(solution)/shard_map/ppermute | solution.py:14
  298.0 24.6 %collective-permute-start.42 = (bf16[128,3072]{1,0:T(8,128)(2,1)S(1)}, bf16[128,3072]{1,0:T(8,128)(2,1)S(1)}, u32[]{:S(2)}, u32[]{:S(2)}) collective-permute-start(bf16[128,3072]{1,0:T(8,128)(2,1)S(1)} %pad_maximum_fusion.10), channel_id=1, source_target_pairs={{0,1},{1,2},{2,3},{3,0},{4,5},{5,6},{6,7},{7,4},{8,9},{9,10},{10,1... | collective-permute-start | bytes 2359304 | tf_op jit(solution)/shard_map/ppermute | solution.py:14
  298.2 33.6 %collective-permute-start.44 = (bf16[128,3072]{1,0:T(8,128)(2,1)S(1)}, bf16[128,3072]{1,0:T(8,128)(2,1)}, u32[]{:S(2)}, u32[]{:S(2)}) collective-permute-start(bf16[128,3072]{1,0:T(8,128)(2,1)S(1)} %pad_maximum_fusion.11), channel_id=1, source_target_pairs={{0,3},{1,0},{2,1},{3,2},{4,7},{5,4},{6,5},{7,6},{8,11},{9,8},{10,9... | collective-permute-start | bytes 2359304 | tf_op jit(solution)/shard_map/ppermute | solution.py:14
  305.8 33.7 %collective-permute-start.31 = (bf16[128,3072]{1,0:T(8,128)(2,1)S(1)}, bf16[128,3072]{1,0:T(8,128)(2,1)S(1)}, u32[]{:S(2)}, u32[]{:S(2)}) collective-permute-start(bf16[128,3072]{1,0:T(8,128)(2,1)S(1)} %pad_maximum_fusion.7), channel_id=1, source_target_pairs={{0,1},{1,2},{2,3},{3,0},{4,5},{5,6},{6,7},{7,4},{8,9},{9,10},{10,1... | collective-permute-start | bytes 2359304 | tf_op jit(solution)/shard_map/ppermute | solution.py:14
  314.9 35.2 %collective-permute-start.33 = (bf16[128,3072]{1,0:T(8,128)(2,1)S(1)}, bf16[128,3072]{1,0:T(8,128)(2,1)S(1)}, u32[]{:S(2)}, u32[]{:S(2)}) collective-permute-start(bf16[128,3072]{1,0:T(8,128)(2,1)S(1)} %pad_maximum_fusion.8), channel_id=1, source_target_pairs={{0,3},{1,0},{2,1},{3,2},{4,7},{5,4},{6,5},{7,6},{8,11},{9,8},{10,9... | collective-permute-start | bytes 2359304 | tf_op jit(solution)/shard_map/ppermute | solution.py:14
  322.6 33.7 %collective-permute-start.9 = (bf16[128,3072]{1,0:T(8,128)(2,1)S(1)}, bf16[128,3072]{1,0:T(8,128)(2,1)S(1)}, u32[]{:S(2)}, u32[]{:S(2)}) collective-permute-start(bf16[128,3072]{1,0:T(8,128)(2,1)S(1)} %pad_maximum_fusion.1), channel_id=1, source_target_pairs={{0,1},{1,2},{2,3},{3,0},{4,5},{5,6},{6,7},{7,4},{8,9},{9,10},{10,1... | collective-permute-start | bytes 2359304 | tf_op jit(solution)/shard_map/ppermute | solution.py:14
  331.8 33.7 %collective-permute-start.11 = (bf16[128,3072]{1,0:T(8,128)(2,1)S(1)}, bf16[128,3072]{1,0:T(8,128)(2,1)S(1)}, u32[]{:S(2)}, u32[]{:S(2)}) collective-permute-start(bf16[128,3072]{1,0:T(8,128)(2,1)S(1)} %pad_maximum_fusion.2), channel_id=1, source_target_pairs={{0,3},{1,0},{2,1},{3,2},{4,7},{5,4},{6,5},{7,6},{8,11},{9,8},{10,9... | collective-permute-start | bytes 2359304 | tf_op jit(solution)/shard_map/ppermute | solution.py:14
  339.5 118.0 %collective-permute-start.55 = (bf16[384,3072]{1,0:T(8,128)(2,1)S(1)}, bf16[384,3072]{1,0:T(8,128)(2,1)S(1)}, u32[]{:S(2)}, u32[]{:S(2)}) collective-permute-start(bf16[384,3072]{1,0:T(8,128)(2,1)S(1)} %copy-done.44), channel_id=1, source_target_pairs={{0,120},{8,112},{16,104},{24,96},{32,88},{40,80},{48,72},{56,64},{... | collective-permute-start | bytes 7077896 | tf_op jit(solution)/shard_map/ppermute | solution.py:14
  350.1 59.0 %collective-permute-start.23 = (bf16[64,3072]{1,0:T(8,128)(2,1)S(1)}, bf16[64,3072]{1,0:T(8,128)(2,1)S(1)}, u32[]{:S(2)}, u32[]{:S(2)}) collective-permute-start(bf16[64,3072]{1,0:T(8,128)(2,1)S(1)} %slice.594), channel_id=1, source_target_pairs={{0,4},{1,5},{2,6},{3,7},{4,0},{5,1},{6,2},{7,3},{8,12},{9,13},{10,... | collective-permute-start | bytes 1179656 | tf_op jit(solution)/shard_map/ppermute | solution.py:14
  350.4 75.5 %copy-start.2 = (bf16[2,1,64,3072]{3,2,1,0:T(8,128)(2,1)S(1)}, bf16[2,1,64,3072]{3,2,1,0:T(8,128)(2,1)}, u32[]{:S(2)}) copy-start(bf16[2,1,64,3072]{3,2,1,0:T(8,128)(2,1)} %param.8) | copy-start | bytes 2359300
  350.4 75.5 %copy-start.29 = (f32[1,1,3072]{2,1,0:T(1,128)S(1)}, f32[1,1,3072]{2,1,0:T(1,128)}, u32[]{:S(2)}) copy-start(f32[1,1,3072]{2,1,0:T(1,128)} %copy-done.28) | copy-start | bytes 36868
  356.4 61.1 %collective-permute-start.45 = (bf16[64,3072]{1,0:T(8,128)(2,1)S(1)}, bf16[64,3072]{1,0:T(8,128)(2,1)S(1)}, u32[]{:S(2)}, u32[]{:S(2)}) collective-permute-start(bf16[64,3072]{1,0:T(8,128)(2,1)S(1)} %slice.592), channel_id=1, source_target_pairs={{0,4},{1,5},{2,6},{3,7},{4,0},{5,1},{6,2},{7,3},{8,12},{9,13},{10,... | collective-permute-start | bytes 1179656 | tf_op jit(solution)/shard_map/ppermute | solution.py:14
  365.5 60.5 %collective-permute-start.34 = (bf16[64,3072]{1,0:T(8,128)(2,1)S(1)}, bf16[64,3072]{1,0:T(8,128)(2,1)S(1)}, u32[]{:S(2)}, u32[]{:S(2)}) collective-permute-start(bf16[64,3072]{1,0:T(8,128)(2,1)S(1)} %slice.593), channel_id=1, source_target_pairs={{0,4},{1,5},{2,6},{3,7},{4,0},{5,1},{6,2},{7,3},{8,12},{9,13},{10,... | collective-permute-start | bytes 1179656 | tf_op jit(solution)/shard_map/ppermute | solution.py:14
  367.0 67.4 %copy-start.4 = (bf16[2,1,64,3072]{3,2,1,0:T(8,128)(2,1)S(1)}, bf16[2,1,64,3072]{3,2,1,0:T(8,128)(2,1)}, u32[]{:S(2)}) copy-start(bf16[2,1,64,3072]{3,2,1,0:T(8,128)(2,1)} %param.10) | copy-start | bytes 2359300
  409.1 25.3 %collective-permute-start.12 = (bf16[64,3072]{1,0:T(8,128)(2,1)S(1)}, bf16[64,3072]{1,0:T(8,128)(2,1)S(1)}, u32[]{:S(2)}, u32[]{:S(2)}) collective-permute-start(bf16[64,3072]{1,0:T(8,128)(2,1)S(1)} %slice.595), channel_id=1, source_target_pairs={{0,4},{1,5},{2,6},{3,7},{4,0},{5,1},{6,2},{7,3},{8,12},{9,13},{10,... | collective-permute-start | bytes 1179656 | tf_op jit(solution)/shard_map/ppermute | solution.py:14
  435.2 17.2 %collective-permute-start.35 = (bf16[64,3072]{1,0:T(8,128)(2,1)S(1)}, bf16[64,3072]{1,0:T(8,128)(2,1)S(1)}, u32[]{:S(2)}, u32[]{:S(2)}) collective-permute-start(bf16[64,3072]{1,0:T(8,128)(2,1)S(1)} %get-tuple-element.78), channel_id=1, source_target_pairs={{0,120},{8,0},{16,8},{24,16},{32,24},{40,32},{48,40},{56,48},{64,5... | collective-permute-start | bytes 1179656 | tf_op jit(solution)/shard_map/ppermute | solution.py:14
  435.7 16.6 %collective-permute-start.46 = (bf16[64,3072]{1,0:T(8,128)(2,1)S(1)}, bf16[64,3072]{1,0:T(8,128)(2,1)S(1)}, u32[]{:S(2)}, u32[]{:S(2)}) collective-permute-start(bf16[64,3072]{1,0:T(8,128)(2,1)S(1)} %get-tuple-element.79), channel_id=1, source_target_pairs={{0,8},{8,16},{16,24},{24,32},{32,40},{40,48},{48,56},{56,64},{64,7... | collective-permute-start | bytes 1179656 | tf_op jit(solution)/shard_map/ppermute | solution.py:14
  438.5 17.4 %collective-permute-start.13 = (bf16[64,3072]{1,0:T(8,128)(2,1)S(1)}, bf16[64,3072]{1,0:T(8,128)(2,1)S(1)}, u32[]{:S(2)}, u32[]{:S(2)}) collective-permute-start(bf16[64,3072]{1,0:T(8,128)(2,1)S(1)} %get-tuple-element.82), channel_id=1, source_target_pairs={{0,8},{8,16},{16,24},{24,32},{32,40},{40,48},{48,56},{56,64},{64,7... | collective-permute-start | bytes 1179656 | tf_op jit(solution)/shard_map/ppermute | solution.py:14
  438.5 18.1 %collective-permute-start.24 = (bf16[64,3072]{1,0:T(8,128)(2,1)S(1)}, bf16[64,3072]{1,0:T(8,128)(2,1)S(1)}, u32[]{:S(2)}, u32[]{:S(2)}) collective-permute-start(bf16[64,3072]{1,0:T(8,128)(2,1)S(1)} %get-tuple-element.83), channel_id=1, source_target_pairs={{0,120},{8,0},{16,8},{24,16},{32,24},{40,32},{48,40},{56,48},{64,5... | collective-permute-start | bytes 1179656 | tf_op jit(solution)/shard_map/ppermute | solution.py:14
  (50 other events, 938.7 us)
